TPU v7x, 32 devices: a whole 2x2x4 slice. The times are simulated.
32 devices in a mesh: db: 8 (over z, core), pb: 4 (over y, x).
Axes of the slice: x: 2, y: 2, z: 4, core: 2. Of those that a mesh axis runs over, the one named last changes fastest.
Arguments:
- queries: bfloat16 [128, 768], P('pb', 'db'), may hold values from -6 to 6
- codebook: float32 [192, 16, 4], P('pb'), may hold values from -0.21875 to 0.21875
- codes: int32 [16384, 192], P('db'), may hold values from 0 to 15
- full_rows: bfloat16 [8192, 768], P('db'), may hold values from -0.21875 to 0.21875
- candidates: int32 [128, 256], P('pb'), may hold values from 0 to 8191, as said below
- location: int32 [8192], replicated, may hold values from 0 to 8191, as said below
Outputs:
- approx_scores: bfloat16 [128, 16384], P('pb', 'db')
- rescored: float32 [128, 256], P('pb', 'db')
Inputs may be any that keep to these rules, and one draw needn't show every extreme that they name: `candidates`: the owner of a candidate is row_of // 1024; among the candidate slots of the 32 queries of one index of pb in the 256 // 8 columns of one index of db, no owner holds more than 256, and one owner holds exactly 256. Each vector id appears once; vector v is row location[v] of full_rows.
All inputs are finite; a program needn't handle non-finite values.
Results may differ from a plain program's by a relative error of at most 0.005.
Values may be sent and summed in bfloat16 or wider, within the bound.
A program may use at most 64 MiB of HBM per device.

v0:
```python
import math

import jax
import jax.numpy as jnp
from jax import lax
from jax.sharding import PartitionSpec as P


def lookup_rows(location, candidates):
    total = location.shape[0]
    width = math.gcd(total, 256)
    height = total // width
    upper = (location // 256).astype(jnp.bfloat16).reshape(height, width)
    lower = (location % 256).astype(jnp.bfloat16).reshape(height, width)
    stacked = jnp.concatenate([upper, lower], axis=1)
    flat_ids = candidates.reshape(-1)
    id_high = flat_ids // width
    id_low = flat_ids % width
    row_hot = (id_high[:, None] == jnp.arange(height, dtype=jnp.int32)[None, :]).astype(
        jnp.bfloat16
    )
    picked_rows = jnp.dot(row_hot, stacked, preferred_element_type=jnp.float32)
    column_hot = id_low[:, None] == jnp.arange(width, dtype=jnp.int32)[None, :]
    upper_val = jnp.sum(jnp.where(column_hot, picked_rows[:, :width], 0.0), axis=1).astype(
        jnp.int32
    )
    lower_val = jnp.sum(jnp.where(column_hot, picked_rows[:, width:], 0.0), axis=1).astype(
        jnp.int32
    )
    return (upper_val * 256 + lower_val).reshape(candidates.shape)


def pick_scores(exact_scores, local_row):
    query_count, full_dev = exact_scores.shape
    group = math.gcd(query_count, 8)
    columns = jnp.arange(full_dev, dtype=jnp.int32)

    def one_group(inputs):
        score_block, row_block = inputs
        match = row_block[:, :, None] == columns[None, None, :]
        return jnp.sum(jnp.where(match, score_block[:, None, :], 0.0), axis=2)

    picked = lax.map(
        one_group,
        (
            exact_scores.reshape(query_count // group, group, full_dev),
            local_row.reshape(query_count // group, group, local_row.shape[1]),
        ),
    )
    return picked.reshape(query_count, local_row.shape[1])


def local(queries, codebook, codes, full_rows, candidates, location):
    codebook_all = lax.all_gather(codebook, "pb", axis=0, tiled=True)
    queries_all = lax.all_gather(queries, "db", axis=1, tiled=True)
    query_count = queries_all.shape[0]
    sub_count, code_count, sub_width = codebook_all.shape
    all_parts = queries_all.astype(jnp.float32).reshape(query_count, sub_count, sub_width)
    lookup_table = jnp.einsum(
        "qsj,scj->qsc", all_parts, codebook_all, precision=lax.Precision.HIGHEST
    )
    lookup_table = lookup_table.reshape(query_count, sub_count * code_count).astype(jnp.bfloat16)
    rows_dev = codes.shape[0]
    block_rows = math.gcd(rows_dev, 512)
    block_count = rows_dev // block_rows
    levels = jnp.arange(code_count, dtype=jnp.int32)

    def scan_block(position, scores_so_far):
        code_block = lax.dynamic_slice_in_dim(codes, position * block_rows, block_rows, 0)
        onehot = (
            (code_block[:, :, None] == levels)
            .astype(jnp.bfloat16)
            .reshape(block_rows, sub_count * code_count)
        )
        block_scores = lax.dot_general(
            lookup_table, onehot, (((1,), (1,)), ((), ())), preferred_element_type=jnp.float32
        )
        return lax.dynamic_update_slice_in_dim(
            scores_so_far, block_scores.astype(jnp.bfloat16), position * block_rows, 1
        )

    approx_scores = lax.fori_loop(
        0, block_count, scan_block, jnp.zeros((query_count, rows_dev), jnp.bfloat16)
    )
    full_dev = full_rows.shape[0]
    exact_scores = lax.dot_general(
        queries_all, full_rows, (((1,), (1,)), ((), ())), preferred_element_type=jnp.float32
    )
    row_of = lookup_rows(location, candidates)
    owners = row_of // full_dev
    local_row = row_of % full_dev
    my_index = lax.axis_index("db")
    mine = owners == my_index
    picked = pick_scores(exact_scores, jnp.where(mine, local_row, full_dev))
    rescored = lax.psum_scatter(picked, "db", scatter_dimension=1, tiled=True)
    return (approx_scores, rescored)


def solution(mesh):
    in_specs = (
        P("pb", "db"),
        P("pb", None, None),
        P("db", None),
        P("db", None),
        P("pb", None),
        P(),
    )
    out_specs = (P("pb", "db"), P("pb", "db"))
    return jax.shard_map(local, mesh=mesh, in_specs=in_specs, out_specs=out_specs, check_vma=False)
```

profile of v0, /device:TPU:0, one launch (start us, length us, event | category | flops | bytes accessed | tf_op | source)
XLA Modules:
  0.0 75.8 jit_solution(16102387069036972119)
XLA Ops:
  7.2 0.0 copy-start
  7.2 0.0 reduce-scatter.4.cloned.1.call-start
  7.2 0.9 %copy.25 = s32[4,2,8,128]{3,1,2,0:T(2,128)S(1)} copy(s32[4,2,8,128]{3,2,1,0:T(8,128)} %bitcast.55) | data formatting | bytes 65536
  8.2 0.8 %fusion.10 = (bf16[8192]{0:T(1024)(128)(2,1)S(1)}, bf16[8192]{0:T(1024)(128)(2,1)S(1)}) fusion(s32[8192]{0:T(1024)} %param.15), kind=kLoop, calls=%fused_computation.37 | loop fusion | flops 172032 | bytes 65536 | tf_op jit(solution)/shard_map/convert_element_type | solution.py:13
  9.0 2.4 %fusion.8 = f32[8192,512]{0,1:T(8,128)S(1)} fusion(s32[8192]{0:T(1024)S(1)} %get-tuple-element.180, bf16[32,256]{1,0:T(8,128)(2,1)S(1)} %reshape.103, bf16[32,256]{1,0:T(8,128)(2,1)S(1)} %reshape.102), kind=kOutput, calls=%fused_computation.20 | convolution fusion | flops 268763136 | bytes 16842752 | tf_op jit(solution)/shard_map/dot_general | solution.py:22
  11.4 0.0 copy-start.3
  11.4 1.8 %fusion.7 = (f32[8192]{0:T(1024)S(1)}, f32[8192]{0:T(1024)S(1)}) fusion(f32[8192,512]{0,1:T(8,128)S(1)} %fusion.8, s32[8192]{0:T(1024)S(1)} %get-tuple-element.179), kind=kLoop, calls=%fused_computation.15 | loop fusion | flops 10469376 | bytes 16875520 | tf_op jit(solution)/shard_map/reduce_sum | solution.py:24
  13.2 0.0 copy-start.2
  13.3 0.0 copy-done.3
  13.3 15.7 %all-gather = bf16[8,96,32]{1,2,0:T(8,128)(2,1)S(1)} all-gather(bf16[1,96,32]{1,2,0:T(8,128)(2,1)S(1)} %bitcast.57), channel_id=1, replica_groups=mesh['db'=8,'pb'=4] {'db'}, dimensions={0}, use_global_device_ids=true | all-gather | bytes 55296 | tf_op jit(solution)/shard_map/all_gather | solution.py:55
  29.0 0.1 reshape.107
  29.1 0.0 copy-done
  29.1 0.5 convolution_bitcast_fusion
  29.7 5.6 %while.26 = (s32[]{:T(128)}, f32[4,8,256]{2,1,0:T(8,128)S(1)}, s32[4,8,256]{2,1,0:T(8,128)S(1)}, f32[4,8,1024]{2,1,0:T(8,128)S(1)}, s32[]{:T(128)}) while((s32[]{:T(128)}, f32[4,8,256]{2,1,0:T(8,128)S(1)}, s32[4,8,256]{2,1,0:T(8,128)S(1)}, f32[4,8,1024]{2,1,0:T(8,128)S(1)}, s32[]{:T(128)}) %tuple.61), condition=%wide.region_6.7_spmd.clone, body=%wide.region_4.6_spmd.clone.sunk | while | flops 6289410 | bytes 147529 | solution.py:43
  29.7 1.3 %select_reduce_fusion.2 = f32[8,256]{1,0:T(8,128)S(1)} fusion(f32[8,1024]{1,0:T(8,128)S(1)} %dynamic-slice_bitcast_fusion.4, s32[8,256]{1,0:T(8,128)S(1)} %dynamic-slice_bitcast_fusion.5), kind=kLoop, calls=%fused_computation.8.clone.1 | loop fusion | flops 6289408 | bytes 49152 | tf_op jit(solution)/shard_map/while/body/eval_jaxpr/reduce_sum | solution.py:41
  31.1 1.3 %select_reduce_fusion.2 = f32[8,256]{1,0:T(8,128)S(1)} fusion(f32[8,1024]{1,0:T(8,128)S(1)} %dynamic-slice_bitcast_fusion.4, s32[8,256]{1,0:T(8,128)S(1)} %dynamic-slice_bitcast_fusion.5), kind=kLoop, calls=%fused_computation.8.clone.1 | loop fusion | flops 6289408 | bytes 49152 | tf_op jit(solution)/shard_map/while/body/eval_jaxpr/reduce_sum | solution.py:41
  32.5 1.3 %select_reduce_fusion.2 = f32[8,256]{1,0:T(8,128)S(1)} fusion(f32[8,1024]{1,0:T(8,128)S(1)} %dynamic-slice_bitcast_fusion.4, s32[8,256]{1,0:T(8,128)S(1)} %dynamic-slice_bitcast_fusion.5), kind=kLoop, calls=%fused_computation.8.clone.1 | loop fusion | flops 6289408 | bytes 49152 | tf_op jit(solution)/shard_map/while/body/eval_jaxpr/reduce_sum | solution.py:41
  33.9 1.3 %select_reduce_fusion.2 = f32[8,256]{1,0:T(8,128)S(1)} fusion(f32[8,1024]{1,0:T(8,128)S(1)} %dynamic-slice_bitcast_fusion.4, s32[8,256]{1,0:T(8,128)S(1)} %dynamic-slice_bitcast_fusion.5), kind=kLoop, calls=%fused_computation.8.clone.1 | loop fusion | flops 6289408 | bytes 49152 | tf_op jit(solution)/shard_map/while/body/eval_jaxpr/reduce_sum | solution.py:41
  35.3 0.8 copy.23
  36.0 0.0 reduce-scatter.4.cloned.1.call-update
  36.1 0.2 copy.21
  36.2 0.0 copy-done.2
  36.2 0.1 copy.19
  36.3 9.5 %all_gather.6 = f32[192,16,4]{1,2,0:T(4,128)S(1)} all-gather(f32[48,16,4]{1,2,0:T(4,128)S(1)} %copy.19), channel_id=1, replica_groups=mesh['db'=8,'pb'=4] {'pb'}, dimensions={0}, use_global_device_ids=true | all-gather | bytes 61440 | tf_op jit(solution)/shard_map/all_gather | solution.py:54
  45.9 1.4 %convolution_convert_fusion.1 = bf16[192,16,32]{2,1,0:T(8,128)(2,1)S(1)} fusion(f32[192,16,4]{1,2,0:T(4,128)S(1)} %all_gather.6, bf16[32,192,4]{0,2,1:T(4,128)(2,1)S(1)} %bitcast.50), kind=kOutput, calls=%fused_computation.17 | convolution fusion | flops 4816896 | bytes 294912 | tf_op jit(solution)/shard_map/qsj,scj->qsc/dot_general | solution.py:59
  47.3 0.3 copy.22
  47.6 12.6 %while.25 = (s32[]{:T(128)}, bf16[32,2048]{1,0:T(8,128)(2,1)S(1)}, s32[2048,192]{0,1:T(8,128)}, bf16[32,3072]{1,0:T(8,128)(2,1)S(1)}, s32[]{:T(128)}, /*index=5*/s32[]{:T(128)}, s32[]{:T(128)}, s32[]{:T(128)}) while((s32[]{:T(128)}, bf16[32,2048]{1,0:T(8,128)(2,1)S(1)}, s32[2048,192]{0,1:T(8,128)}, bf16[32,3072]{1,0:T(8,128)(2,1)S(1)}, ...), condition=%wide.region_1.0_spmd.clone, body=%wide.region_0.0_spmd.clone.sunk | while | flops 102252552 | bytes 4604043 | solution.py:82
  47.6 1.0 %constant_dynamic-slice_fusion.2 = s32[512,192]{0,1:T(8,128)S(1)} fusion(s32[2048,192]{0,1:T(8,128)} %get-tuple-element.251, s32[]{:T(128)S(6)} %select_n.101), kind=kLoop, calls=%fused_computation.6.clone.1 | loop fusion | bytes 786436 | tf_op jit(solution)/shard_map/while/body/eval_jaxpr/dynamic_slice | solution.py:69
  48.7 0.1 eq.147
  48.8 1.1 %bitcast_compare_fusion.2 = pred[512,3072]{0,1:T(32,128)(4,1)S(1)} fusion(s32[3072]{0:T(1024)S(1)} %eq.147, s32[512,192]{0,1:T(8,128)S(1)} %constant_dynamic-slice_fusion.2), kind=kLoop, calls=%fused_computation.2.clone.1 | loop fusion | flops 1572864 | bytes 1978368 | tf_op jit(solution)/shard_map/while/body/eval_jaxpr/eq | solution.py:71
  49.9 0.9 %fusion.35 = bf16[32,2048]{1,0:T(8,128)(2,1)S(1)} fusion(bf16[32,2048]{1,0:T(8,128)(2,1)S(1)} %get-tuple-element.242, s32[]{:T(128)S(6)} %select_n.101, pred[512,3072]{0,1:T(32,128)(4,1)S(1)} %bitcast_compare_fusion.2, bf16[32,3072]{1,0:T(8,128)(2,1)S(1)} %get-tuple-element.252), kind=kOutput, calls=%fused_computation.5.clone.1 | convolution fusion | flops 100679680 | bytes 1802244 | tf_op jit(solution)/shard_map/while/body/eval_jaxpr/dot_general | solution.py:75
  50.8 1.0 %constant_dynamic-slice_fusion.2 = s32[512,192]{0,1:T(8,128)S(1)} fusion(s32[2048,192]{0,1:T(8,128)} %get-tuple-element.251, s32[]{:T(128)S(6)} %select_n.101), kind=kLoop, calls=%fused_computation.6.clone.1 | loop fusion | bytes 786436 | tf_op jit(solution)/shard_map/while/body/eval_jaxpr/dynamic_slice | solution.py:69
  51.8 0.1 eq.147
  51.9 1.1 %bitcast_compare_fusion.2 = pred[512,3072]{0,1:T(32,128)(4,1)S(1)} fusion(s32[3072]{0:T(1024)S(1)} %eq.147, s32[512,192]{0,1:T(8,128)S(1)} %constant_dynamic-slice_fusion.2), kind=kLoop, calls=%fused_computation.2.clone.1 | loop fusion | flops 1572864 | bytes 1978368 | tf_op jit(solution)/shard_map/while/body/eval_jaxpr/eq | solution.py:71
  53.0 0.9 %fusion.35 = bf16[32,2048]{1,0:T(8,128)(2,1)S(1)} fusion(bf16[32,2048]{1,0:T(8,128)(2,1)S(1)} %get-tuple-element.242, s32[]{:T(128)S(6)} %select_n.101, pred[512,3072]{0,1:T(32,128)(4,1)S(1)} %bitcast_compare_fusion.2, bf16[32,3072]{1,0:T(8,128)(2,1)S(1)} %get-tuple-element.252), kind=kOutput, calls=%fused_computation.5.clone.1 | convolution fusion | flops 100679680 | bytes 1802244 | tf_op jit(solution)/shard_map/while/body/eval_jaxpr/dot_general | solution.py:75
  53.9 1.0 %constant_dynamic-slice_fusion.2 = s32[512,192]{0,1:T(8,128)S(1)} fusion(s32[2048,192]{0,1:T(8,128)} %get-tuple-element.251, s32[]{:T(128)S(6)} %select_n.101), kind=kLoop, calls=%fused_computation.6.clone.1 | loop fusion | bytes 786436 | tf_op jit(solution)/shard_map/while/body/eval_jaxpr/dynamic_slice | solution.py:69
  54.9 0.1 eq.147
  55.0 1.1 %bitcast_compare_fusion.2 = pred[512,3072]{0,1:T(32,128)(4,1)S(1)} fusion(s32[3072]{0:T(1024)S(1)} %eq.147, s32[512,192]{0,1:T(8,128)S(1)} %constant_dynamic-slice_fusion.2), kind=kLoop, calls=%fused_computation.2.clone.1 | loop fusion | flops 1572864 | bytes 1978368 | tf_op jit(solution)/shard_map/while/body/eval_jaxpr/eq | solution.py:71
  56.2 0.9 %fusion.35 = bf16[32,2048]{1,0:T(8,128)(2,1)S(1)} fusion(bf16[32,2048]{1,0:T(8,128)(2,1)S(1)} %get-tuple-element.242, s32[]{:T(128)S(6)} %select_n.101, pred[512,3072]{0,1:T(32,128)(4,1)S(1)} %bitcast_compare_fusion.2, bf16[32,3072]{1,0:T(8,128)(2,1)S(1)} %get-tuple-element.252), kind=kOutput, calls=%fused_computation.5.clone.1 | convolution fusion | flops 100679680 | bytes 1802244 | tf_op jit(solution)/shard_map/while/body/eval_jaxpr/dot_general | solution.py:75
  57.0 1.0 %constant_dynamic-slice_fusion.2 = s32[512,192]{0,1:T(8,128)S(1)} fusion(s32[2048,192]{0,1:T(8,128)} %get-tuple-element.251, s32[]{:T(128)S(6)} %select_n.101), kind=kLoop, calls=%fused_computation.6.clone.1 | loop fusion | bytes 786436 | tf_op jit(solution)/shard_map/while/body/eval_jaxpr/dynamic_slice | solution.py:69
  58.1 0.1 eq.147
  58.2 1.1 %bitcast_compare_fusion.2 = pred[512,3072]{0,1:T(32,128)(4,1)S(1)} fusion(s32[3072]{0:T(1024)S(1)} %eq.147, s32[512,192]{0,1:T(8,128)S(1)} %constant_dynamic-slice_fusion.2), kind=kLoop, calls=%fused_computation.2.clone.1 | loop fusion | flops 1572864 | bytes 1978368 | tf_op jit(solution)/shard_map/while/body/eval_jaxpr/eq | solution.py:71
  59.3 0.9 %fusion.35 = bf16[32,2048]{1,0:T(8,128)(2,1)S(1)} fusion(bf16[32,2048]{1,0:T(8,128)(2,1)S(1)} %get-tuple-element.242, s32[]{:T(128)S(6)} %select_n.101, pred[512,3072]{0,1:T(32,128)(4,1)S(1)} %bitcast_compare_fusion.2, bf16[32,3072]{1,0:T(8,128)(2,1)S(1)} %get-tuple-element.252), kind=kOutput, calls=%fused_computation.5.clone.1 | convolution fusion | flops 100679680 | bytes 1802244 | tf_op jit(solution)/shard_map/while/body/eval_jaxpr/dot_general | solution.py:75
  60.2 0.0 copy-start.1
  60.2 7.4 %reduce-scatter.4.cloned.1.call-done = f32[32,32]{1,0:T(8,128)} async-done(((f32[256,32]{1,0:T(8,128)}), f32[32,32]{1,0:T(8,128)}) %reduce-scatter.4.cloned.1.call-update) | async-done | bytes 4112
  67.6 1.4 %copy.24 = f32[32,32]{1,0:T(8,128)} copy(f32[32,32]{0,1:T(8,128)} %bitcast.56) | data formatting | bytes 8192
  69.0 0.0 copy-done.1
  (25 shorter events, 0.3 us)
Async XLA Ops:
  7.2 21.9 %copy-start = (bf16[1024,768]{1,0:T(8,128)(2,1)S(1)}, bf16[1024,768]{1,0:T(8,128)(2,1)}, u32[]{:S(2)}) copy-start(bf16[1024,768]{1,0:T(8,128)(2,1)} %param.13) | copy-start | bytes 4718596
  7.2 60.4 %reduce-scatter.4.cloned.1.call-start = ((), (), s32[]{:S(2)}) async-start(), calls=%async_computation.1 | async-start | bytes 147456
  11.4 1.9 %copy-start.3 = (bf16[32,96]{1,0:T(8,128)(2,1)S(1)}, bf16[32,96]{1,0:T(8,128)(2,1)}, u32[]{:S(2)}) copy-start(bf16[32,96]{1,0:T(8,128)(2,1)} %param.10) | copy-start | bytes 18436
  13.2 23.0 %copy-start.2 = (f32[48,16,4]{0,2,1:T(4,128)S(1)}, f32[48,16,4]{0,2,1:T(4,128)}, u32[]{:S(2)}) copy-start(f32[48,16,4]{0,2,1:T(4,128)} %param.11) | copy-start | bytes 36868
  60.2 8.8 %copy-start.1 = (bf16[32,2048]{1,0:T(8,128)(2,1)}, bf16[32,2048]{1,0:T(8,128)(2,1)S(1)}, u32[]{:S(2)}) copy-start(bf16[32,2048]{1,0:T(8,128)(2,1)S(1)} %get-tuple-element.121) | copy-start | bytes 393220
Sparse Core Ops, SparseCore 0:
  36.2 31.3 reduce-scatter.3
where the time goes:
time: 76.3 us; the launch traced here: 75.8 us
  blocking collectives  25.2 us (33%)
  between operations  14.2 us (19%)
  other arithmetic  12.5 us (16%)
  local copies, waits for them, and re-layouts  8.39 us (11%)
  matrix products  7.81 us (10%)
  waiting for transfers between devices  7.39 us (10%)
    all_gather x1, blocking collectives, local(): queries_all = lax.all_gather(queries, 'db', axis=1, tiled=True)  15.7 us
    all_gather x1, blocking collectives, local(): codebook_all = lax.all_gather(codebook, 'pb', axis=0, tiled=True)  9.53 us
    unnamed x2, waiting for transfers between devices  7.39 us
    reduce_sum x4, other arithmetic, one_group(): return jnp.sum(jnp.where(match, score_block[:, None, :], 0.0), axis=2)  5.32 us
    eq x4, other arithmetic, scan_block(): code_block[:, :, None] == levels  4.52 us
    dynamic_slice x4, local copies, waits for them, and re-layouts, scan_block(): lax.dynamic_slice_in_dim(codes, position * block_rows, block_rows, 0)  4.12 us
    unnamed x15, local copies, waits for them, and re-layouts  3.69 us
    dot_general x4, matrix products, scan_block(): lax.dot_general(lookup_table, onehot, (((1,), (1,)), ((), ())), preferred...  3.44 us
  transfers between devices with their start and end apart: 1, of which 1 were waited for; matrix products, arithmetic and copies ran while one was open for 19% of the time, Pallas kernels for 0%

commit v1 on v0

v1 whole, which is shorter than its diff:
```python
import functools

import jax
import jax.numpy as jnp
from jax import lax
from jax.experimental import pallas as pl
from jax.experimental.pallas import tpu as pltpu
from jax.sharding import PartitionSpec as P

LANES = 128
SUBLANES = 8
CHUNK = 256


def pick_lanes(table, index):
    return jnp.take_along_axis(table, index, axis=1, mode="promise_in_bounds")


def dot_last(a, b):
    return lax.dot_general(a, b, (((1,), (1,)), ((), ())), preferred_element_type=jnp.float32)


def kernel(
    n_db, n_pb,
    q_hbm, cb_hbm, codes_hbm, full_hbm, cand_hbm, loc_hbm,
    approx_ref, resc_ref,
    q_slots, cb_slots, codes_v, full_v, cand_v, loc_v, perm_v, flat_v, table_v, dec_v, row_v, sent_v, got_v,
    local_sem, q_send, q_recv, cb_send, cb_recv, s_send, s_recv,
):
    my_db = lax.axis_index("db")
    my_pb = lax.axis_index("pb")
    query_count, part = q_hbm.shape
    code_count, sub_width, sub_part = cb_hbm.shape
    sub_count, rows_dev = codes_hbm.shape
    full_dev, width = full_hbm.shape
    cand_count = cand_hbm.shape[1]
    db_peers = [lax.rem(my_db + step, n_db) for step in range(1, n_db)]
    pb_peers = [lax.rem(my_pb + step, n_pb) for step in range(1, n_pb)]

    def on_device(src, dst, k):
        copy = pltpu.make_async_copy(src, dst, local_sem.at[k])
        copy.start()
        return copy

    barrier = pltpu.get_barrier_semaphore()
    for peer in db_peers:
        pl.semaphore_signal(barrier, inc=1, device_id={"db": peer}, device_id_type=pl.DeviceIdType.MESH)
    for peer in pb_peers:
        pl.semaphore_signal(barrier, inc=1, device_id={"pb": peer}, device_id_type=pl.DeviceIdType.MESH)
    get_loc = on_device(loc_hbm, loc_v, 0)
    get_cand = on_device(cand_hbm, cand_v, 1)
    get_q = on_device(q_hbm, q_slots.at[my_db], 2)
    get_cb = on_device(cb_hbm, cb_slots.at[my_pb], 3)
    get_full = on_device(full_hbm, full_v, 4)
    get_codes = on_device(codes_hbm, codes_v, 5)
    pl.semaphore_wait(barrier, n_db + n_pb - 2)

    def send_queries(peer, slot):
        return pltpu.make_async_remote_copy(
            src_ref=q_hbm, dst_ref=q_slots.at[slot], send_sem=q_send.at[peer], recv_sem=q_recv.at[slot],
            device_id={"db": peer}, device_id_type=pl.DeviceIdType.MESH)

    def send_codebook(peer, slot):
        return pltpu.make_async_remote_copy(
            src_ref=cb_hbm, dst_ref=cb_slots.at[slot], send_sem=cb_send.at[peer], recv_sem=cb_recv.at[slot],
            device_id={"pb": peer}, device_id_type=pl.DeviceIdType.MESH)

    def send_scores(peer, slot):
        return pltpu.make_async_remote_copy(
            src_ref=sent_v.at[peer], dst_ref=got_v.at[slot], send_sem=s_send.at[peer], recv_sem=s_recv.at[slot],
            device_id={"db": peer}, device_id_type=pl.DeviceIdType.MESH)

    for peer in db_peers:
        send_queries(peer, my_db).start()
    for peer in pb_peers:
        send_codebook(peer, my_pb).start()

    halves = cand_count // LANES
    get_loc.wait()
    get_cand.wait()
    ids = [cand_v[:, h * LANES:(h + 1) * LANES] for h in range(halves)]
    highs = [jnp.right_shift(x, 7) for x in ids]
    lows = [jnp.bitwise_and(x, LANES - 1) for x in ids]

    def lookup(step, found):
        block = loc_v[pl.ds(pl.multiple_of(step * SUBLANES, SUBLANES), SUBLANES), :]
        found = list(found)
        for r in range(SUBLANES):
            row = jnp.broadcast_to(block[r:r + 1, :], (query_count, LANES))
            for h in range(halves):
                found[h] = jnp.where(highs[h] == step * SUBLANES + r, pick_lanes(row, lows[h]), found[h])
        return tuple(found)

    zero = jnp.zeros((query_count, LANES), jnp.int32)
    found = lax.fori_loop(0, loc_hbm.shape[0] // SUBLANES, lookup, (zero,) * halves)
    for h in range(halves):
        row_v[:, h * LANES:(h + 1) * LANES] = found[h] - my_db * full_dev

    column = lax.broadcasted_iota(jnp.int32, (1, width), 1)
    member = jnp.zeros((1, width), jnp.int32)
    for j in range(1, sub_width):
        member = member + jnp.where(column >= j * sub_count, 1, 0)
    feature = (column - member * sub_count) * sub_width + member
    perm_v[...] = jnp.where(
        lax.broadcasted_iota(jnp.int32, (width, width), 0) == feature, 1.0, 0.0).astype(jnp.bfloat16)

    get_q.wait()
    for peer in db_peers:
        send_queries(peer, peer).wait_recv()
    queries = jnp.concatenate(
        [q_slots[i].astype(jnp.float32) for i in range(n_db)], axis=1).astype(jnp.bfloat16)
    get_full.wait()
    exact = dot_last(queries, full_v[...])
    picked = []
    for h in range(halves):
        row = row_v[:, h * LANES:(h + 1) * LANES]
        high = jnp.right_shift(row, 7)
        low = jnp.bitwise_and(row, LANES - 1)
        score = jnp.zeros((query_count, LANES), jnp.float32)
        for t in range(full_dev // LANES):
            score = jnp.where(high == t, pick_lanes(exact[:, t * LANES:(t + 1) * LANES], low), score)
        picked.append(score)

    block = cand_count // n_db
    groups = query_count // SUBLANES
    group_of = lax.broadcasted_iota(jnp.int32, (SUBLANES, LANES), 1) // block
    for b in range(n_db):
        half, offset = (b * block) // LANES, (b * block) % LANES
        packed = jnp.zeros((SUBLANES, LANES), jnp.float32)
        for g in range(groups):
            piece = picked[half][g * SUBLANES:(g + 1) * SUBLANES, :]
            shift = (g * block - offset) % LANES
            if shift:
                piece = pltpu.roll(piece, shift, 1)
            packed = jnp.where(group_of == g, piece, packed)
        sent_v[b] = packed
    for peer in db_peers:
        send_scores(peer, my_db).start()

    permuted = jnp.dot(queries, perm_v[...], preferred_element_type=jnp.float32).astype(jnp.bfloat16)
    get_cb.wait()
    for peer in pb_peers:
        send_codebook(peer, peer).wait_recv()
    used = code_count * sub_width
    eye = jnp.where(
        lax.broadcasted_iota(jnp.int32, (sub_part, sub_part), 0)
        == lax.broadcasted_iota(jnp.int32, (sub_part, sub_part), 1), 1.0, 0.0).astype(jnp.bfloat16)
    for i in range(n_pb):
        for c in range(code_count):
            flat_v[i, c * sub_width:(c + 1) * sub_width, :] = cb_slots[i, c]
        flat_v[i, used:, :] = jnp.zeros((LANES - used, sub_part), jnp.float32)
        table_v[i * sub_part:(i + 1) * sub_part, :] = dot_last(eye, flat_v[i].astype(jnp.bfloat16))
    get_codes.wait()

    def scan(step, carry):
        for k in range(2):
            start = pl.multiple_of((step * 2 + k) * CHUNK, CHUNK)
            for h in range(CHUNK // LANES):
                code = codes_v[:, pl.ds(start + h * LANES, LANES)] * sub_width
                for j in range(sub_width):
                    dec_v[k, j * sub_count:(j + 1) * sub_count, h * LANES:(h + 1) * LANES] = pick_lanes(
                        table_v[...], code + j).astype(jnp.bfloat16)
            scores = jnp.dot(permuted, dec_v[k], preferred_element_type=jnp.float32)
            approx_ref[:, pl.ds(start, CHUNK)] = scores.astype(approx_ref.dtype)
        return carry

    lax.fori_loop(0, rows_dev // (2 * CHUNK), scan, 0)

    total = sent_v[my_db]
    for peer in db_peers:
        send_scores(peer, peer).wait_recv()
        total = total + got_v[peer]
    for g in range(groups):
        shift = (-g * block) % LANES
        resc_ref[g * SUBLANES:(g + 1) * SUBLANES, :] = (pltpu.roll(total, shift, 1) if shift else total)[:, :block]
    for peer in db_peers:
        send_queries(peer, my_db).wait_send()
        send_scores(peer, my_db).wait_send()
    for peer in pb_peers:
        send_codebook(peer, my_pb).wait_send()


def local(n_db, n_pb, queries, codebook, codes, full_rows, candidates, location):
    codebook_t = jnp.transpose(codebook, (1, 2, 0))
    codes_t = codes.T
    location_rows = location.reshape(-1, LANES)
    query_count, part = queries.shape
    sub_part, code_count, sub_width = codebook.shape
    rows_dev, sub_count = codes.shape
    full_dev, width = full_rows.shape
    cand_count = candidates.shape[1]
    assert query_count * (cand_count // n_db) <= SUBLANES * LANES
    return pl.pallas_call(
        functools.partial(kernel, n_db, n_pb),
        out_shape=(
            jax.ShapeDtypeStruct((query_count, rows_dev), jnp.bfloat16),
            jax.ShapeDtypeStruct((query_count, cand_count // n_db), jnp.float32),
        ),
        in_specs=[pl.BlockSpec(memory_space=pl.ANY)] * 6,
        out_specs=[pl.BlockSpec(memory_space=pltpu.VMEM)] * 2,
        scratch_shapes=[
            pltpu.VMEM((n_db, query_count, part), jnp.bfloat16),
            pltpu.VMEM((n_pb, code_count, sub_width, sub_part), jnp.float32),
            pltpu.VMEM((sub_count, rows_dev), jnp.int32),
            pltpu.VMEM((full_dev, width), jnp.bfloat16),
            pltpu.VMEM((query_count, cand_count), jnp.int32),
            pltpu.VMEM(location_rows.shape, jnp.int32),
            pltpu.VMEM((width, width), jnp.bfloat16),
            pltpu.VMEM((n_pb, LANES, sub_part), jnp.float32),
            pltpu.VMEM((sub_count, LANES), jnp.float32),
            pltpu.VMEM((2, width, CHUNK), jnp.bfloat16),
            pltpu.VMEM((query_count, cand_count), jnp.int32),
            pltpu.VMEM((n_db, SUBLANES, LANES), jnp.float32),
            pltpu.VMEM((n_db, SUBLANES, LANES), jnp.float32),
            pltpu.SemaphoreType.DMA((6,)),
            pltpu.SemaphoreType.DMA((n_db,)),
            pltpu.SemaphoreType.DMA((n_db,)),
            pltpu.SemaphoreType.DMA((n_pb,)),
            pltpu.SemaphoreType.DMA((n_pb,)),
            pltpu.SemaphoreType.DMA((n_db,)),
            pltpu.SemaphoreType.DMA((n_db,)),
        ],
        compiler_params=pltpu.CompilerParams(
            collective_id=0, has_side_effects=True, vmem_limit_bytes=60 * 1024 * 1024),
    )(queries, codebook_t, codes_t, full_rows, candidates, location_rows)


def solution(mesh):
    in_specs = (
        P("pb", "db"),
        P("pb", None, None),
        P("db", None),
        P("db", None),
        P("pb", None),
        P(),
    )
    out_specs = (P("pb", "db"), P("pb", "db"))
    sizes = mesh.shape
    return jax.shard_map(
        functools.partial(local, sizes["db"], sizes["pb"]),
        mesh=mesh, in_specs=in_specs, out_specs=out_specs, check_vma=False)
```

time: 76.3 us -> 21.3 us (0.28)
  blocking collectives: 25.2 us -> 0 us
  Pallas kernels: 0 us -> 17.6 us
  between operations: 14.2 us -> 0.64 us
  other arithmetic: 12.5 us -> 0 us
  matrix products: 7.81 us -> 0 us
  waiting for transfers between devices: 7.39 us -> 0 us
  local copies, waits for them, and re-layouts: 8.39 us -> 2.89 us
    all_gather x2 -> x0, blocking collectives: 25.2 us -> none  [the longest x1 15.7 us: local(): queries_all = lax.all_gather(queries, 'db', axis=1, tiled=True)]
    pallas_call x0 -> x1, Pallas kernels: none -> 17.6 us  [local(): pl.pallas_call(functools.partial(kernel, n_db, n_pb), out_shape=(jax.Shap...]
    dot_general x7 -> x0, matrix products: 7.81 us -> none  [the longest x4 3.44 us: scan_block(): lax.dot_general(lookup_table, onehot, (((1,), (1,)), ((), ())), preferred...]
    unnamed x2 -> x0, waiting for transfers between devices: 7.39 us -> none
    reduce_sum x5 -> x0, other arithmetic: 7.13 us -> none  [the longest x4 5.32 us: one_group(): return jnp.sum(jnp.where(match, score_block[:, None, :], 0.0), axis=2)]
    eq x4 -> x0, other arithmetic: 4.52 us -> none  [scan_block(): code_block[:, :, None] == levels]
    dynamic_slice x4 -> x0, local copies, waits for them, and re-layouts: 4.12 us -> none  [scan_block(): lax.dynamic_slice_in_dim(codes, position * block_rows, block_rows, 0)]
    unnamed x15 -> x2, local copies, waits for them, and re-layouts: 3.69 us -> 2.89 us
  transfers between devices with their start and end apart: 1 -> 0, of which waited for: 1 -> 0; matrix products, arithmetic and copies ran while one was open for 19% -> 0% of each run, Pallas kernels for 0% -> 0%
where the time goes in v1:
time: 21.3 us; the launch traced here: 21.1 us
  Pallas kernels  17.6 us (83%)
  local copies, waits for them, and re-layouts  2.89 us (14%)
  between operations  0.64 us (3%)
    pallas_call x1, Pallas kernels, local(): pl.pallas_call(functools.partial(kernel, n_db, n_pb), out_shape=(jax.Shap...  17.6 us
    unnamed x2, local copies, waits for them, and re-layouts  2.89 us

profile of v1, /device:TPU:0, one launch (start us, length us, event | category | flops | bytes accessed | tf_op | source)
XLA Modules:
  0.0 21.1 jit_solution(14241433560623508283)
XLA Ops:
  0.6 17.6 %shard_map.77 = (bf16[32,2048]{1,0:T(8,128)(2,1)}, f32[32,32]{1,0:T(8,128)}) custom-call(bf16[32,96]{1,0:T(8,128)(2,1)} %q_hbm.1, f32[16,4,48]{2,1,0:T(4,128)} %bitcast.4, s32[192,2048]{1,0:T(8,128)} %bitcast.3, bf16[1024,768]{1,0:T(8,128)(2,1)} %full_hbm.1, s32[32,256]{1,0:T(8,128)} %cand_hbm.1, s32[64,128]{1,0:T(8,128)} %bitcast.5), custom_call_target="tpu_custom_call" | custom-call | tf_op jit(solution)/shard_map/pallas_call | solution.py:193
  18.2 1.6 %copy.10 = bf16[32,2048]{1,0:T(8,128)(2,1)} copy(bf16[32,2048]{1,0:T(8,128)(2,1)} %get-tuple-element.4) | data formatting | bytes 262144
  19.8 1.3 %copy.11 = f32[32,32]{1,0:T(8,128)} copy(f32[32,32]{1,0:T(8,128)} %get-tuple-element.5) | data formatting | bytes 8192

commit v2 on v1

--- a/solution.py
+++ b/solution.py
@@ -24,7 +24,7 @@
     n_db, n_pb,
     q_hbm, cb_hbm, codes_hbm, full_hbm, cand_hbm, loc_hbm,
     approx_ref, resc_ref,
-    q_slots, cb_slots, codes_v, full_v, cand_v, loc_v, perm_v, flat_v, table_v, dec_v, row_v, sent_v, got_v,
+    q_slots, cb_slots, codes_v, full_v, cand_v, loc_v, perm_v, flat_v, table_v, dec_v, row_v, exact_v, sent_v, got_v,
     local_sem, q_send, q_recv, cb_send, cb_recv, s_send, s_recv,
 ):
     my_db = lax.axis_index("db")
@@ -53,48 +53,6 @@
     get_cb = on_device(cb_hbm, cb_slots.at[my_pb], 3)
     get_full = on_device(full_hbm, full_v, 4)
     get_codes = on_device(codes_hbm, codes_v, 5)
-    pl.semaphore_wait(barrier, n_db + n_pb - 2)
-
-    def send_queries(peer, slot):
-        return pltpu.make_async_remote_copy(
-            src_ref=q_hbm, dst_ref=q_slots.at[slot], send_sem=q_send.at[peer], recv_sem=q_recv.at[slot],
-            device_id={"db": peer}, device_id_type=pl.DeviceIdType.MESH)
-
-    def send_codebook(peer, slot):
-        return pltpu.make_async_remote_copy(
-            src_ref=cb_hbm, dst_ref=cb_slots.at[slot], send_sem=cb_send.at[peer], recv_sem=cb_recv.at[slot],
-            device_id={"pb": peer}, device_id_type=pl.DeviceIdType.MESH)
-
-    def send_scores(peer, slot):
-        return pltpu.make_async_remote_copy(
-            src_ref=sent_v.at[peer], dst_ref=got_v.at[slot], send_sem=s_send.at[peer], recv_sem=s_recv.at[slot],
-            device_id={"db": peer}, device_id_type=pl.DeviceIdType.MESH)
-
-    for peer in db_peers:
-        send_queries(peer, my_db).start()
-    for peer in pb_peers:
-        send_codebook(peer, my_pb).start()
-
-    halves = cand_count // LANES
-    get_loc.wait()
-    get_cand.wait()
-    ids = [cand_v[:, h * LANES:(h + 1) * LANES] for h in range(halves)]
-    highs = [jnp.right_shift(x, 7) for x in ids]
-    lows = [jnp.bitwise_and(x, LANES - 1) for x in ids]
-
-    def lookup(step, found):
-        block = loc_v[pl.ds(pl.multiple_of(step * SUBLANES, SUBLANES), SUBLANES), :]
-        found = list(found)
-        for r in range(SUBLANES):
-            row = jnp.broadcast_to(block[r:r + 1, :], (query_count, LANES))
-            for h in range(halves):
-                found[h] = jnp.where(highs[h] == step * SUBLANES + r, pick_lanes(row, lows[h]), found[h])
-        return tuple(found)
-
-    zero = jnp.zeros((query_count, LANES), jnp.int32)
-    found = lax.fori_loop(0, loc_hbm.shape[0] // SUBLANES, lookup, (zero,) * halves)
-    for h in range(halves):
-        row_v[:, h * LANES:(h + 1) * LANES] = found[h] - my_db * full_dev
 
     column = lax.broadcasted_iota(jnp.int32, (1, width), 1)
     member = jnp.zeros((1, width), jnp.int32)
@@ -104,22 +62,69 @@
     perm_v[...] = jnp.where(
         lax.broadcasted_iota(jnp.int32, (width, width), 0) == feature, 1.0, 0.0).astype(jnp.bfloat16)
 
+    pl.semaphore_wait(barrier, n_db + n_pb - 2)
+
+    def send_queries(peer, slot):
+        return pltpu.make_async_remote_copy(
+            src_ref=q_hbm, dst_ref=q_slots.at[slot], send_sem=q_send.at[peer], recv_sem=q_recv.at[slot],
+            device_id={"db": peer}, device_id_type=pl.DeviceIdType.MESH)
+
+    def send_codebook(peer, slot):
+        return pltpu.make_async_remote_copy(
+            src_ref=cb_hbm, dst_ref=cb_slots.at[slot], send_sem=cb_send.at[peer], recv_sem=cb_recv.at[slot],
+            device_id={"pb": peer}, device_id_type=pl.DeviceIdType.MESH)
+
+    def send_scores(peer, slot):
+        return pltpu.make_async_remote_copy(
+            src_ref=sent_v.at[peer], dst_ref=got_v.at[slot], send_sem=s_send.at[peer], recv_sem=s_recv.at[slot],
+            device_id={"db": peer}, device_id_type=pl.DeviceIdType.MESH)
+
+    for peer in db_peers:
+        send_queries(peer, my_db).start()
+    for peer in pb_peers:
+        send_codebook(peer, my_pb).start()
+
+    halves = cand_count // LANES
+    get_loc.wait()
+    get_cand.wait()
+    spots = [(g, h) for g in range(query_count // SUBLANES) for h in range(halves)]
+    views = [(slice(g * SUBLANES, (g + 1) * SUBLANES), slice(h * LANES, (h + 1) * LANES)) for g, h in spots]
+    highs = [jnp.right_shift(cand_v[view], 7) for view in views]
+    lows = [jnp.bitwise_and(cand_v[view], LANES - 1) for view in views]
+
+    def lookup(step, found):
+        first = step * SUBLANES
+        block = loc_v[pl.ds(pl.multiple_of(first, SUBLANES), SUBLANES), :]
+        rows = [jnp.broadcast_to(block[r:r + 1, :], (SUBLANES, LANES)) for r in range(SUBLANES)]
+        out = []
+        for value, high, low in zip(found, highs, lows):
+            for r, row in enumerate(rows):
+                value = jnp.where(high == first + r, pick_lanes(row, low), value)
+            out.append(value)
+        return tuple(out)
+
+    zero = jnp.zeros((SUBLANES, LANES), jnp.int32)
+    found = lax.fori_loop(0, loc_hbm.shape[0] // SUBLANES, lookup, (zero,) * len(views))
+    for view, value in zip(views, found):
+        row_v[view] = value - my_db * full_dev
+
     get_q.wait()
     for peer in db_peers:
         send_queries(peer, peer).wait_recv()
     queries = jnp.concatenate(
         [q_slots[i].astype(jnp.float32) for i in range(n_db)], axis=1).astype(jnp.bfloat16)
     get_full.wait()
-    exact = dot_last(queries, full_v[...])
-    picked = []
-    for h in range(halves):
-        row = row_v[:, h * LANES:(h + 1) * LANES]
+    exact_v[...] = dot_last(queries, full_v[...])
+    picked = {}
+    for (g, h), view in zip(spots, views):
+        row = row_v[view]
         high = jnp.right_shift(row, 7)
         low = jnp.bitwise_and(row, LANES - 1)
-        score = jnp.zeros((query_count, LANES), jnp.float32)
+        score = jnp.zeros((SUBLANES, LANES), jnp.float32)
         for t in range(full_dev // LANES):
-            score = jnp.where(high == t, pick_lanes(exact[:, t * LANES:(t + 1) * LANES], low), score)
-        picked.append(score)
+            tile = exact_v[view[0], t * LANES:(t + 1) * LANES]
+            score = jnp.where(high == t, pick_lanes(tile, low), score)
+        picked[g, h] = score
 
     block = cand_count // n_db
     groups = query_count // SUBLANES
@@ -128,7 +133,7 @@
         half, offset = (b * block) // LANES, (b * block) % LANES
         packed = jnp.zeros((SUBLANES, LANES), jnp.float32)
         for g in range(groups):
-            piece = picked[half][g * SUBLANES:(g + 1) * SUBLANES, :]
+            piece = picked[g, half]
             shift = (g * block - offset) % LANES
             if shift:
                 piece = pltpu.roll(piece, shift, 1)
@@ -147,19 +152,23 @@
         == lax.broadcasted_iota(jnp.int32, (sub_part, sub_part), 1), 1.0, 0.0).astype(jnp.bfloat16)
     for i in range(n_pb):
         for c in range(code_count):
-            flat_v[i, c * sub_width:(c + 1) * sub_width, :] = cb_slots[i, c]
+            flat_v[i, pl.ds(c, sub_width, stride=code_count), :] = cb_slots[i, c]
         flat_v[i, used:, :] = jnp.zeros((LANES - used, sub_part), jnp.float32)
-        table_v[i * sub_part:(i + 1) * sub_part, :] = dot_last(eye, flat_v[i].astype(jnp.bfloat16))
+        table_v[0, i * sub_part:(i + 1) * sub_part, :] = dot_last(eye, flat_v[i].astype(jnp.bfloat16))
+    for j in range(1, sub_width):
+        table_v[j] = pltpu.roll(table_v[0], LANES - j * code_count, 1)
     get_codes.wait()
 
     def scan(step, carry):
         for k in range(2):
             start = pl.multiple_of((step * 2 + k) * CHUNK, CHUNK)
             for h in range(CHUNK // LANES):
-                code = codes_v[:, pl.ds(start + h * LANES, LANES)] * sub_width
-                for j in range(sub_width):
-                    dec_v[k, j * sub_count:(j + 1) * sub_count, h * LANES:(h + 1) * LANES] = pick_lanes(
-                        table_v[...], code + j).astype(jnp.bfloat16)
+                for s in range(0, sub_count, 2 * SUBLANES):
+                    code = codes_v[s:s + 2 * SUBLANES, pl.ds(start + h * LANES, LANES)]
+                    for j in range(sub_width):
+                        values = pick_lanes(table_v[j, s:s + 2 * SUBLANES, :], code)
+                        dec_v[k, j * sub_count + s:j * sub_count + s + 2 * SUBLANES, h * LANES:(h + 1) * LANES] = (
+                            values.astype(jnp.bfloat16))
             scores = jnp.dot(permuted, dec_v[k], preferred_element_type=jnp.float32)
             approx_ref[:, pl.ds(start, CHUNK)] = scores.astype(approx_ref.dtype)
         return carry
@@ -178,6 +187,17 @@
         send_scores(peer, my_db).wait_send()
     for peer in pb_peers:
         send_codebook(peer, my_pb).wait_send()
+
+
+def write_out(approx_ref, resc_ref, approx_hbm, resc_hbm, sem):
+    copies = [
+        pltpu.make_async_copy(approx_ref, approx_hbm, sem.at[0]),
+        pltpu.make_async_copy(resc_ref, resc_hbm, sem.at[1]),
+    ]
+    for copy in copies:
+        copy.start()
+    for copy in copies:
+        copy.wait()
 
 
 def local(n_db, n_pb, queries, codebook, codes, full_rows, candidates, location):
@@ -190,13 +210,13 @@
     full_dev, width = full_rows.shape
     cand_count = candidates.shape[1]
     assert query_count * (cand_count // n_db) <= SUBLANES * LANES
-    return pl.pallas_call(
+    approx, resc = pl.pallas_call(
         functools.partial(kernel, n_db, n_pb),
         out_shape=(
-            jax.ShapeDtypeStruct((query_count, rows_dev), jnp.bfloat16),
-            jax.ShapeDtypeStruct((query_count, cand_count // n_db), jnp.float32),
+            pltpu.VMEM((query_count, rows_dev), jnp.bfloat16),
+            pltpu.VMEM((query_count, cand_count // n_db), jnp.float32),
         ),
-        in_specs=[pl.BlockSpec(memory_space=pl.ANY)] * 6,
+        in_specs=[pl.BlockSpec(memory_space=pltpu.HBM)] * 6,
         out_specs=[pl.BlockSpec(memory_space=pltpu.VMEM)] * 2,
         scratch_shapes=[
             pltpu.VMEM((n_db, query_count, part), jnp.bfloat16),
@@ -207,9 +227,10 @@
             pltpu.VMEM(location_rows.shape, jnp.int32),
             pltpu.VMEM((width, width), jnp.bfloat16),
             pltpu.VMEM((n_pb, LANES, sub_part), jnp.float32),
-            pltpu.VMEM((sub_count, LANES), jnp.float32),
+            pltpu.VMEM((sub_width, sub_count, LANES), jnp.float32),
             pltpu.VMEM((2, width, CHUNK), jnp.bfloat16),
             pltpu.VMEM((query_count, cand_count), jnp.int32),
+            pltpu.VMEM((query_count, full_dev), jnp.float32),
             pltpu.VMEM((n_db, SUBLANES, LANES), jnp.float32),
             pltpu.VMEM((n_db, SUBLANES, LANES), jnp.float32),
             pltpu.SemaphoreType.DMA((6,)),
@@ -223,6 +244,16 @@
         compiler_params=pltpu.CompilerParams(
             collective_id=0, has_side_effects=True, vmem_limit_bytes=60 * 1024 * 1024),
     )(queries, codebook_t, codes_t, full_rows, candidates, location_rows)
+    return pl.pallas_call(
+        write_out,
+        out_shape=(
+            jax.ShapeDtypeStruct((query_count, rows_dev), jnp.bfloat16),
+            jax.ShapeDtypeStruct((query_count, cand_count // n_db), jnp.float32),
+        ),
+        in_specs=[pl.BlockSpec(memory_space=pltpu.VMEM)] * 2,
+        out_specs=[pl.BlockSpec(memory_space=pltpu.HBM)] * 2,
+        scratch_shapes=[pltpu.SemaphoreType.DMA((2,))],
+    )(approx, resc)
 
 
 def solution(mesh):

time: 21.3 us -> 18.5 us (0.87)
  local copies, waits for them, and re-layouts: 2.89 us -> 1.25 us
  Pallas kernels: 17.6 us -> 16.5 us
    unnamed x2 -> x4, local copies, waits for them, and re-layouts: 2.89 us -> 1.25 us
    pallas_call x1 -> x2, Pallas kernels: 17.6 us -> 16.5 us  [the longest x1 14.9 us: local(): pl.pallas_call(functools.partial(kernel, n_db, n_pb), out_shape=(pltpu.VM...]
where the time goes in v2:
time: 18.5 us; the launch traced here: 18.4 us
  Pallas kernels  16.5 us (89%)
  local copies, waits for them, and re-layouts  1.25 us (7%)
  between operations  0.65 us (4%)
    pallas_call x1, Pallas kernels, local(): pl.pallas_call(functools.partial(kernel, n_db, n_pb), out_shape=(pltpu.VM...  14.9 us
    pallas_call x1, Pallas kernels, local(): pl.pallas_call(write_out, out_shape=(jax.ShapeDtypeStruct((query_count, r...  1.58 us
    unnamed x4, local copies, waits for them, and re-layouts  1.25 us

profile of v2, /device:TPU:0, one launch (start us, length us, event | category | flops | bytes accessed | tf_op | source)
XLA Modules:
  0.0 18.4 jit_solution(6068438285885575626)
XLA Ops:
  0.6 14.9 %shard_map.77 = (bf16[32,2048]{1,0:T(8,128)(2,1)S(1)}, f32[32,32]{1,0:T(8,128)S(1)}) custom-call(bf16[32,96]{1,0:T(8,128)(2,1)} %q_hbm.1, f32[16,4,48]{2,1,0:T(4,128)} %bitcast.4, s32[192,2048]{1,0:T(8,128)} %bitcast.3, bf16[1024,768]{1,0:T(8,128)(2,1)} %full_hbm.1, s32[32,256]{1,0:T(8,128)} %cand_hbm.1, s32[64,128]{1,0:T(8,128)} %bitcast.5), custom_call_target="tpu_custom_call" | custom-call | tf_op jit(solution)/shard_map/pallas_call | solution.py:213
  15.5 0.0 copy-start
  15.5 0.6 %copy-done = bf16[32,2048]{1,0:T(8,128)(2,1)} copy-done((bf16[32,2048]{1,0:T(8,128)(2,1)}, bf16[32,2048]{1,0:T(8,128)(2,1)S(1)}, u32[]{:S(2)}) %copy-start) | copy-done | bytes 131096
  16.2 0.0 copy-start.1
  16.2 0.6 %copy-done.1 = f32[32,32]{1,0:T(8,128)} copy-done((f32[32,32]{1,0:T(8,128)}, f32[32,32]{1,0:T(8,128)S(1)}, u32[]{:S(2)}) %copy-start.1) | copy-done | bytes 4120
  16.8 1.6 %shard_map.78 = (bf16[32,2048]{1,0:T(8,128)(2,1)}, f32[32,32]{1,0:T(8,128)}) custom-call(bf16[32,2048]{1,0:T(8,128)(2,1)} %copy-done, f32[32,32]{1,0:T(8,128)} %copy-done.1), custom_call_target="tpu_custom_call" | custom-call | tf_op jit(solution)/shard_map/pallas_call | solution.py:247
Async XLA Ops:
  15.5 0.6 %copy-start = (bf16[32,2048]{1,0:T(8,128)(2,1)}, bf16[32,2048]{1,0:T(8,128)(2,1)S(1)}, u32[]{:S(2)}) copy-start(bf16[32,2048]{1,0:T(8,128)(2,1)S(1)} %get-tuple-element.4.approx_ref) | copy-start | bytes 393220
  16.2 0.6 %copy-start.1 = (f32[32,32]{1,0:T(8,128)}, f32[32,32]{1,0:T(8,128)S(1)}, u32[]{:S(2)}) copy-start(f32[32,32]{1,0:T(8,128)S(1)} %get-tuple-element.5.resc_ref) | copy-start | bytes 12292

commit v3 on v2

--- a/solution.py
+++ b/solution.py
@@ -253,6 +253,7 @@
         in_specs=[pl.BlockSpec(memory_space=pltpu.VMEM)] * 2,
         out_specs=[pl.BlockSpec(memory_space=pltpu.HBM)] * 2,
         scratch_shapes=[pltpu.SemaphoreType.DMA((2,))],
+        compiler_params=pltpu.CompilerParams(vmem_limit_bytes=1024 * 1024),
     )(approx, resc)
 
 

time: 18.5 us -> 16.3 us (0.88)
  local copies, waits for them, and re-layouts: 1.25 us -> 0 us
  Pallas kernels: 16.5 us -> 15.6 us
    unnamed x4 -> x0, local copies, waits for them, and re-layouts: 1.25 us -> none
    pallas_call x1, Pallas kernels: 1.58 us -> 0.68 us  [local(): pl.pallas_call(write_out, out_shape=(jax.ShapeDtypeStruct((query_count, r...]
where the time goes in v3:
time: 16.3 us; the launch traced here: 16.2 us
  Pallas kernels  15.6 us (96%)
  between operations  0.64 us (4%)
    pallas_call x1, Pallas kernels, local(): pl.pallas_call(functools.partial(kernel, n_db, n_pb), out_shape=(pltpu.VM...  14.9 us
    pallas_call x1, Pallas kernels, local(): pl.pallas_call(write_out, out_shape=(jax.ShapeDtypeStruct((query_count, r...  0.68 us

profile of v3, /device:TPU:0, one launch (start us, length us, event | category | flops | bytes accessed | tf_op | source)
XLA Modules:
  0.0 16.2 jit_solution(8480548644003695928)
XLA Ops:
  0.6 14.9 %shard_map.77 = (bf16[32,2048]{1,0:T(8,128)(2,1)S(1)}, f32[32,32]{1,0:T(8,128)S(1)}) custom-call(bf16[32,96]{1,0:T(8,128)(2,1)} %q_hbm.1, f32[16,4,48]{2,1,0:T(4,128)} %bitcast.4, s32[192,2048]{1,0:T(8,128)} %bitcast.3, bf16[1024,768]{1,0:T(8,128)(2,1)} %full_hbm.1, s32[32,256]{1,0:T(8,128)} %cand_hbm.1, s32[64,128]{1,0:T(8,128)} %bitcast.5), custom_call_target="tpu_custom_call" | custom-call | tf_op jit(solution)/shard_map/pallas_call | solution.py:213
  15.5 0.7 %shard_map.78 = (bf16[32,2048]{1,0:T(8,128)(2,1)}, f32[32,32]{1,0:T(8,128)}) custom-call(bf16[32,2048]{1,0:T(8,128)(2,1)S(1)} %get-tuple-element.4.approx_ref, f32[32,32]{1,0:T(8,128)S(1)} %get-tuple-element.5.resc_ref), custom_call_target="tpu_custom_call" | custom-call | tf_op jit(solution)/shard_map/pallas_call | solution.py:247
